TPU v7x, 256 devices: a whole 4x4x8 slice. The times are simulated.
256 devices in a mesh: dp: 8 (over z_lo, x), vocab: 32 (over y, z_hi, core).
Axes of the slice: x: 4, y: 4, z: 8 (z_hi: 4, z_lo: 2; z = z_hi * 2 + z_lo), core: 2. Of those that a mesh axis runs over, the one named last changes fastest.
Arguments:
- hidden_now: bfloat16 [1024, 3584], P('dp'), may hold values from -6 to 6
- hidden_next: bfloat16 [1024, 3584], P('dp'), may hold values from -100 to 100
- cotangent: bfloat16 [1024, 81920], P('dp', 'vocab'), may hold values from -6 to 6
- master: float32 [81920, 3584], P(('vocab', 'dp')), may hold values from -1 to 1
- moment: bfloat16 [81920, 3584], P(('vocab', 'dp')), may hold values from -19.2 to 19.2
- second: bfloat16 [81920, 3584], P(('vocab', 'dp')), may hold values from 2.048 to 20.48, as said below
- targets: int32 [1024], P('dp'), may hold values from 0 to 81919
Outputs:
- next_logits: bfloat16 [1024, 81920], P('dp', 'vocab')
- next_loss: float32 [1024], P('dp')
Inputs may be any that keep to these rules, and one draw needn't show every extreme that they name: `second`: Positive.
All inputs are finite; a program needn't handle non-finite values.
Results may differ from a plain program's by a relative error of at most 0.015.
Values may be sent and summed in bfloat16 or wider, within the bound.
No kernel may reach another device: no remote copies, remote signals or barrier semaphores. Data moves between devices by JAX's collectives and lax.ppermute only.
A program may use at most 128 MiB of HBM per device.

v0:
```python
import jax
import jax.numpy as jnp
from jax import lax
from jax.sharding import PartitionSpec as P

learn_rate = 0.02
beta_one = 0.9
beta_two = 0.95
epsilon = 1e-08
decay_rate = 0.1


def shards(hidden_now, hidden_next, cotangent, master, moment, second, targets):
    partial_grad = lax.dot_general(
        cotangent, hidden_now, (((0,), (0,)), ((), ())), preferred_element_type=jnp.float32
    )
    gradient = lax.psum_scatter(
        partial_grad.astype(jnp.bfloat16), "dp", scatter_dimension=0, tiled=True
    ).astype(jnp.float32)
    moment_new = beta_one * moment.astype(jnp.float32) + (1.0 - beta_one) * gradient
    second_new = beta_two * second.astype(jnp.float32) + (1.0 - beta_two) * gradient * gradient
    master_new = master - learn_rate * (
        moment_new / (jnp.sqrt(second_new) + epsilon) + decay_rate * master
    )
    head_rows = master_new.astype(jnp.bfloat16)
    owner_logits = lax.dot_general(
        lax.all_gather(hidden_next, "dp", axis=0, tiled=True),
        head_rows,
        (((1,), (1,)), ((), ())),
        preferred_element_type=jnp.float32,
    )
    logits = lax.all_to_all(
        owner_logits.astype(jnp.bfloat16), "dp", split_axis=0, concat_axis=1, tiled=True
    ).astype(owner_logits.dtype)
    offset = lax.axis_index("vocab") * logits.shape[1]
    local_target = targets - offset
    positions = lax.broadcasted_iota(jnp.int32, logits.shape, 1)
    picked = jnp.sum(jnp.where(positions == local_target[:, None], logits, 0.0), axis=1)
    row_top = lax.pmax(jnp.max(logits, axis=1), "vocab")
    local_total = jnp.sum(jnp.exp(logits - row_top[:, None]), axis=1)
    row_total, target_logit = lax.psum((local_total, picked), "vocab")
    row_loss = jnp.log(row_total) + row_top - target_logit
    next_rows = logits.astype(jnp.bfloat16)
    return (next_rows, row_loss)


def solution(mesh):
    in_specs = (
        P("dp", None),
        P("dp", None),
        P("dp", "vocab"),
        P(("vocab", "dp"), None),
        P(("vocab", "dp"), None),
        P(("vocab", "dp"), None),
        P("dp"),
    )
    out_specs = (P("dp", "vocab"), P("dp"))
    return jax.shard_map(shards, mesh=mesh, in_specs=in_specs, out_specs=out_specs, check_vma=False)
```

profile of v0, /device:TPU:1, one launch (start us, length us, event | category | flops | bytes accessed | tf_op | source)
XLA Modules:
  0.0 467.6 jit_solution(5824811596226031601)
XLA Ops:
  7.2 0.0 copy-start
  7.2 0.0 all-gather.2.cloned.1.call-start
  7.2 0.7 all-gather.2.cloned.1.call-update
  7.9 0.0 reduce-scatter.2.cloned.1.call-start
  8.0 0.4 copy-done
  8.3 10.0 %convolution_convert_fusion = bf16[2560,3584]{1,0:T(8,128)(2,1)} fusion(bf16[128,2560]{1,0:T(8,128)(2,1)} %param.9, bf16[128,3584]{1,0:T(8,128)(2,1)S(1)} %copy-done), kind=kOutput, calls=%fused_computation | convolution fusion | flops 2357985280 | bytes 19922944 | tf_op jit(solution)/shard_map/dot_general | solution.py:14
  18.3 0.0 copy-start.1
  18.3 0.0 reduce-scatter.2.cloned.1.call-update
  18.4 0.0 copy-start.2
  18.4 79.9 %all-gather.2.cloned.1.call-done = bf16[1024,3584]{1,0:T(8,128)(2,1)} async-done(((bf16[128,3584]{1,0:T(8,128)(2,1)}), bf16[1024,3584]{1,0:T(8,128)(2,1)}) %all-gather.2.cloned.1.call-update) | async-done | bytes 7340048 | tf_op jit(solution)/shard_map/all_gather | solution.py:27
  98.3 190.2 %reduce-scatter.2.cloned.1.call-done = bf16[320,3584]{1,0:T(8,128)(2,1)} async-done(((bf16[2560,3584]{1,0:T(8,128)(2,1)}), bf16[320,3584]{1,0:T(8,128)(2,1)}) %reduce-scatter.2.cloned.1.call-update) | async-done | bytes 2293776 | tf_op jit(solution)/shard_map/reduce_scatter | solution.py:17
  288.5 0.0 copy-done.1
  288.5 10.7 %fusion.17 = bf16[40,8,8,128]{3,2,1,0:T(8,128)(2,1)S(1)} fusion(bf16[1024,3584]{1,0:T(8,128)(2,1)} %all-gather.2.cloned.1.call-done, f32[320,3584]{1,0:T(8,128)} %param.10, bf16[320,3584]{1,0:T(8,128)(2,1)S(1)} %copy-done.1, bf16[320,3584]{1,0:T(8,128)(2,1)} %reduce-scatter.2.cloned.1.call-done, bf16[320,3584]{1,0:T(8,128)(2,1)} %param.11), kind=kOutput, calls=%fused_computation.19 | convolution fusion | flops 2368634880 | bytes 19464192 | tf_op jit(solution)/shard_map/dot_general | solution.py:26
  299.2 1.0 copy.14
  300.2 3.5 all-to-all-start
  303.7 0.0 copy-done.2
  303.8 9.9 %all-to-all-done = bf16[8,128,320]{1,2,0:T(8,128)(2,1)S(1)} async-done(((bf16[8,128,320]{1,2,0:T(8,128)(2,1)}), bf16[8,128,320]{1,2,0:T(8,128)(2,1)S(1)}, u32[]{:S(2)}, u32[]{:S(2)}) %all-to-all-start) | async-done | bytes 655392 | tf_op jit(solution)/shard_map/all_to_all | solution.py:32
  313.7 0.4 reduce_max.14
  314.1 70.8 %pmax.7 = f32[128]{0:T(128)S(1)} all-reduce(bf16[128]{0:T(256)(128)(2,1)S(1)} %reduce_max.14), channel_id=1, replica_groups=mesh['dp'=8,'vocab'=32] {'vocab'}, use_global_device_ids=true, to_apply=%region_2.3 | all-reduce | flops 128 | bytes 768 | tf_op jit(solution)/shard_map/pmax | solution.py:39
  384.8 1.1 copy.11
  385.9 0.5 fusion.15
  386.4 73.8 %all-reduce = (f32[128]{0:T(128)S(1)}, f32[128]{0:T(128)S(1)}) all-reduce(f32[128]{0:T(128)S(1)} %get-tuple-element.5, f32[128]{0:T(128)S(1)} %get-tuple-element.4), channel_id=1, replica_groups=mesh['dp'=8,'vocab'=32] {'vocab'}, use_global_device_ids=true, to_apply=%region_6.7 | all-reduce | flops 256 | bytes 2048 | tf_op jit(solution)/shard_map/psum | solution.py:41
  460.3 0.5 add_subtract_fusion
  (2 shorter events, 0.0 us)
Async XLA Ops:
  7.2 1.2 copy-start
  7.2 91.1 %all-gather.2.cloned.1.call-start = ((), (), s32[]{:S(2)}) async-start(), calls=%async_computation.3 | async-start | bytes 8257536 | tf_op jit(solution)/shard_map/all_gather | solution.py:27
  7.9 280.6 %reduce-scatter.2.cloned.1.call-start = ((), (), s32[]{:S(2)}) async-start(), calls=%async_computation.2 | async-start | bytes 20643840 | tf_op jit(solution)/shard_map/reduce_scatter | solution.py:17
  18.3 270.1 %copy-start.1 = (bf16[320,3584]{1,0:T(8,128)(2,1)S(1)}, bf16[320,3584]{1,0:T(8,128)(2,1)}, u32[]{:S(2)}) copy-start(bf16[320,3584]{1,0:T(8,128)(2,1)} %param.12) | copy-start | bytes 6881284
  18.4 285.4 %copy-start.2 = (s32[128]{0:T(128)S(1)}, s32[128]{0:T(128)}, u32[]{:S(2)}) copy-start(s32[128]{0:T(128)} %param.13) | copy-start | bytes 1540
  300.2 13.5 %all-to-all-start = ((bf16[8,128,320]{1,2,0:T(8,128)(2,1)}), bf16[8,128,320]{1,2,0:T(8,128)(2,1)S(1)}, u32[]{:S(2)}, u32[]{:S(2)}) async-start(bf16[8,128,320]{1,2,0:T(8,128)(2,1)} %bitcast.13), calls=%async_computation.1 | async-start | bytes 1310720 | tf_op jit(solution)/shard_map/all_to_all | solution.py:32
Sparse Core Ops, SparseCore 0:
  9.8 88.4 all-gather.1
  100.9 187.4 reduce-scatter.1
where the time goes:
time: 468 us
  waiting for transfers between devices  281 us (60%)
  blocking collectives  145 us (31%)
  matrix products  20.7 us (4%)
  between operations  14.1 us (3%)
    reduce_scatter x1, waiting for transfers between devices, shards(): lax.psum_scatter(partial_grad.astype(jnp.bfloat16), 'dp', scatter_dimensi...  190 us
    all_gather x1, waiting for transfers between devices, shards(): lax.all_gather(hidden_next, 'dp', axis=0, tiled=True)  79.9 us
    psum x1, blocking collectives, shards(): row_total, target_logit = lax.psum((local_total, picked), 'vocab')  73.8 us
    pmax x1, blocking collectives, shards(): row_top = lax.pmax(jnp.max(logits, axis=1), 'vocab')  70.8 us
    dot_general x1, matrix products, shards(): lax.dot_general(lax.all_gather(hidden_next, 'dp', axis=0, tiled=True), he...  10.7 us
    dot_general x1, matrix products, shards(): lax.dot_general(cotangent, hidden_now, (((0,), (0,)), ((), ())), preferre...  9.99 us
    all_to_all x1, waiting for transfers between devices, shards(): lax.all_to_all(owner_logits.astype(jnp.bfloat16), 'dp', split_axis=0, con...  9.95 us
  transfers between devices with their start and end apart: 3, of which 3 were waited for; matrix products, arithmetic and copies ran while one was open for 2% of the time, Pallas kernels for 0%

commit v1 on v0

--- a/solution.py
+++ b/solution.py
@@ -29,8 +29,14 @@
         (((1,), (1,)), ((), ())),
         preferred_element_type=jnp.float32,
     )
-    logits = lax.all_to_all(
-        owner_logits.astype(jnp.bfloat16), "dp", split_axis=0, concat_axis=1, tiled=True
+    logits = jnp.concatenate(
+        lax.all_to_all(
+            jnp.stack(jnp.split(owner_logits.astype(jnp.bfloat16), lax.axis_size("dp"), axis=0)),
+            "dp",
+            0,
+            0,
+        ),
+        axis=1,
     ).astype(owner_logits.dtype)
     offset = lax.axis_index("vocab") * logits.shape[1]
     local_target = targets - offset

time: 468 us -> 472 us (level)
  no operation moved by 1% of the time
where the time goes in v1:
time: 472 us
  waiting for transfers between devices  281 us (60%)
  blocking collectives  145 us (31%)
  matrix products  20.7 us (4%)
  between operations  14.1 us (3%)
  local copies, waits for them, and re-layouts  6.75 us (1%)
    reduce_scatter x1, waiting for transfers between devices, shards(): lax.psum_scatter(partial_grad.astype(jnp.bfloat16), 'dp', scatter_dimensi...  190 us
    all_gather x1, waiting for transfers between devices, shards(): lax.all_gather(hidden_next, 'dp', axis=0, tiled=True)  79.9 us
    psum x1, blocking collectives, shards(): row_total, target_logit = lax.psum((local_total, picked), 'vocab')  73.8 us
    pmax x1, blocking collectives, shards(): row_top = lax.pmax(jnp.max(logits, axis=1), 'vocab')  70.8 us
    dot_general x1, matrix products, shards(): lax.dot_general(lax.all_gather(hidden_next, 'dp', axis=0, tiled=True), he...  10.7 us
    dot_general x1, matrix products, shards(): lax.dot_general(cotangent, hidden_now, (((0,), (0,)), ((), ())), preferre...  9.99 us
    all_to_all x1, waiting for transfers between devices, shards(): lax.all_to_all(jnp.stack(jnp.split(owner_logits.astype(jnp.bfloat16), lax...  9.95 us
  transfers between devices with their start and end apart: 3, of which 3 were waited for; matrix products, arithmetic and copies ran while one was open for 2% of the time, Pallas kernels for 0%

profile of v1, /device:TPU:1, one launch (start us, length us, event | category | flops | bytes accessed | tf_op | source)
XLA Modules:
  0.0 471.9 jit_solution(8952991758790575644)
XLA Ops:
  7.2 0.0 all-gather.2.cloned.1.call-start
  7.2 0.7 all-gather.2.cloned.1.call-update
  7.9 0.0 reduce-scatter.2.cloned.1.call-start
  8.0 0.4 copy-done
  8.3 10.0 %convolution_convert_fusion = bf16[2560,3584]{1,0:T(8,128)(2,1)} fusion(bf16[128,2560]{1,0:T(8,128)(2,1)} %param.9, bf16[128,3584]{1,0:T(8,128)(2,1)S(1)} %copy-done), kind=kOutput, calls=%fused_computation | convolution fusion | flops 2357985280 | bytes 19922944 | tf_op jit(solution)/shard_map/dot_general | solution.py:14
  18.4 79.9 %all-gather.2.cloned.1.call-done = bf16[1024,3584]{1,0:T(8,128)(2,1)} async-done(((bf16[128,3584]{1,0:T(8,128)(2,1)}), bf16[1024,3584]{1,0:T(8,128)(2,1)}) %all-gather.2.cloned.1.call-update) | async-done | bytes 7340048 | tf_op jit(solution)/shard_map/all_gather | solution.py:27
  98.3 190.2 %reduce-scatter.2.cloned.1.call-done = bf16[320,3584]{1,0:T(8,128)(2,1)} async-done(((bf16[2560,3584]{1,0:T(8,128)(2,1)}), bf16[320,3584]{1,0:T(8,128)(2,1)}) %reduce-scatter.2.cloned.1.call-update) | async-done | bytes 2293776 | tf_op jit(solution)/shard_map/reduce_scatter | solution.py:17
  288.5 10.7 %fusion.17 = bf16[1024,320]{0,1:T(8,128)(2,1)S(1)} fusion(bf16[1024,3584]{1,0:T(8,128)(2,1)} %all-gather.2.cloned.1.call-done, f32[320,3584]{1,0:T(8,128)} %param.10, bf16[320,3584]{1,0:T(8,128)(2,1)S(1)} %copy-done.1, bf16[320,3584]{1,0:T(8,128)(2,1)} %reduce-scatter.2.cloned.1.call-done, bf16[320,3584]{1,0:T(8,128)(2,1)} %param.11), kind=kOutput, calls=%fused_computation.19 | convolution fusion | flops 2368634880 | bytes 19464192 | tf_op jit(solution)/shard_map/dot_general | solution.py:26
  299.2 0.7 fusion.27
  299.9 0.7 fusion.26
  300.5 0.7 fusion.25
  301.2 0.7 fusion.24
  301.9 0.7 fusion.23
  302.5 0.7 fusion.22
  303.2 0.7 fusion.21
  303.8 0.7 fusion.20
  304.5 3.5 all-to-all-start
  308.1 9.9 %all-to-all-done = bf16[8,128,320]{1,2,0:T(8,128)(2,1)S(1)} async-done(((bf16[8,128,320]{1,2,0:T(8,128)(2,1)}), bf16[8,128,320]{1,2,0:T(8,128)(2,1)S(1)}, u32[]{:S(2)}, u32[]{:S(2)}) %all-to-all-start) | async-done | bytes 655392 | tf_op jit(solution)/shard_map/all_to_all | solution.py:33
  318.0 0.4 reduce_max.14
  318.4 70.8 %pmax.7 = f32[128]{0:T(128)S(1)} all-reduce(bf16[128]{0:T(256)(128)(2,1)S(1)} %reduce_max.14), channel_id=1, replica_groups=mesh['dp'=8,'vocab'=32] {'vocab'}, use_global_device_ids=true, to_apply=%region_2.3 | all-reduce | flops 128 | bytes 768 | tf_op jit(solution)/shard_map/pmax | solution.py:45
  389.2 1.1 copy.9
  390.2 0.5 fusion.15
  390.8 73.8 %all-reduce = (f32[128]{0:T(128)S(1)}, f32[128]{0:T(128)S(1)}) all-reduce(f32[128]{0:T(128)S(1)} %get-tuple-element.5, f32[128]{0:T(128)S(1)} %get-tuple-element.4), channel_id=1, replica_groups=mesh['dp'=8,'vocab'=32] {'vocab'}, use_global_device_ids=true, to_apply=%region_6.7 | all-reduce | flops 256 | bytes 2048 | tf_op jit(solution)/shard_map/psum | solution.py:47
  464.6 0.5 add_subtract_fusion
  (8 shorter events, 0.0 us)
Async XLA Ops:
  7.2 1.2 copy-start
  7.2 91.1 %all-gather.2.cloned.1.call-start = ((), (), s32[]{:S(2)}) async-start(), calls=%async_computation.3 | async-start | bytes 8257536 | tf_op jit(solution)/shard_map/all_gather | solution.py:27
  7.9 280.6 %reduce-scatter.2.cloned.1.call-start = ((), (), s32[]{:S(2)}) async-start(), calls=%async_computation.2 | async-start | bytes 20643840 | tf_op jit(solution)/shard_map/reduce_scatter | solution.py:17
  18.3 270.1 %copy-start.1 = (bf16[320,3584]{1,0:T(8,128)(2,1)S(1)}, bf16[320,3584]{1,0:T(8,128)(2,1)}, u32[]{:S(2)}) copy-start(bf16[320,3584]{1,0:T(8,128)(2,1)} %param.12) | copy-start | bytes 6881284
  18.4 289.7 %copy-start.2 = (s32[128]{0:T(128)S(1)}, s32[128]{0:T(128)}, u32[]{:S(2)}) copy-start(s32[128]{0:T(128)} %param.13) | copy-start | bytes 1540
  304.5 13.5 %all-to-all-start = ((bf16[8,128,320]{1,2,0:T(8,128)(2,1)}), bf16[8,128,320]{1,2,0:T(8,128)(2,1)S(1)}, u32[]{:S(2)}, u32[]{:S(2)}) async-start(bf16[8,128,320]{1,2,0:T(8,128)(2,1)} %fusion.20), calls=%async_computation.1 | async-start | bytes 1310720 | tf_op jit(solution)/shard_map/all_to_all | solution.py:33
Sparse Core Ops, SparseCore 0:
  9.8 88.4 all-gather.1
  100.9 187.4 reduce-scatter.1
